TPU v7x, 32 devices: a whole 2x2x4 slice. The times are simulated.
32 devices in a mesh: ta: 4 (over y, x), gz: 4 (over z), col: 2 (over core).
Axes of the slice: x: 2, y: 2, z: 4, core: 2. Of those that a mesh axis runs over, the one named last changes fastest.
Arguments:
- rhs_field: float32 [1, 96, 32, 16, 128], P(None, None, ('ta', 'col'), 'gz'), may hold values from -6 to 6
- link_weights: float32 [8, 32, 16, 128], P(None, ('ta', 'col'), 'gz'), may hold values from 0.4 to 1.6
- fine_blocks: float32 [9, 96, 96], replicated, may hold values from -1 to 5
- smoother: float32 [96, 96], replicated, may hold values from -1 to 1
- plane_next: int32 [4, 128], replicated, may hold values from 0 to 127, as said below
- aggregate: int32 [128], replicated, may hold values from 0 to 7, as said below
- restrict_map: float32 [96, 128], replicated, may hold values from -0.625 to 0.625
- prolong_map: float32 [128, 96], replicated, may hold values from -0.5 to 0.5
- coarse_blocks: float32 [9, 128, 128], replicated, may hold values from -1 to 5
- coarse_smoother: float32 [128, 128], replicated, may hold values from -1 to 1
- coarse_next: int32 [4, 8], replicated, may hold values from 0 to 7, as said below
Outputs:
- solution: float32 [1, 96, 32, 16, 128], P(None, None, ('ta', 'col'), 'gz')
- residual: float32 [1, 96, 32, 16, 128], P(None, None, ('ta', 'col'), 'gz')
Inputs may be any that keep to these rules, and one draw needn't show every extreme that they name: `plane_next`: each row is an ordering of the plane sites; row 1 undoes row 0 and row 3 undoes row 2. `aggregate`: each coarse plane site is named by exactly 16 entries. `coarse_next`: each row is an ordering of the coarse plane sites; row 1 undoes row 0 and row 3 undoes row 2.
All inputs are finite; a program needn't handle non-finite values.
Results may differ from a plain program's by a relative error of at most 0.0003.
Values sent between devices are 32-bit elements; how exact they have to be, the bound alone decides.
A program may use at most 64 MiB of HBM per device.

v0:
```python
import functools

import jax
import jax.numpy as jnp
from jax import lax
from jax.experimental import pallas as pl
from jax.experimental.pallas import tpu as pltpu
from jax.sharding import PartitionSpec as P

SWEEPS = 3
POST = 2
F32 = jnp.float32
BF16 = jnp.bfloat16
MESH = pl.DeviceIdType.MESH
NN = (((1,), (0,)), ((), ()))
NT = (((1,), (1,)), ((), ()))


def dot(a, b, dims=NN):
    return lax.dot_general(a, b, dims, preferred_element_type=F32)


def split(x):
    hi = x.astype(BF16)
    return hi, (x - hi.astype(F32)).astype(BF16)


def stacked(x, axis):
    return jnp.concatenate(split(x), axis=axis)


def left_product(pair, x, dims=NN):
    rows = pair.shape[0] // 2
    hi, lo = split(x)
    both = dot(pair, hi, dims)
    return both[:rows] + both[rows:] + dot(pair[:rows], lo, dims)


def right_product(x, pair):
    columns = pair.shape[1] // 2
    hi, lo = split(x)
    both = dot(hi, pair)
    return both[:, :columns] + both[:, columns:] + dot(lo, pair[:, :columns])


def kernel(
    sizes,
    rhs_ref, weight_ref, blocks_ref, smoother_ref, next_ref, aggregate_ref,
    restrict_ref, prolong_ref, coarse_ref, coarse_smoother_ref, coarse_next_ref,
    solution_ref, residual_ref,
    fields, values, solved, rest, coarse_rhs,
    near_pair, hop_pair, smooth_pair, shuffle, spread,
    restrict_pair, prolong_pair, coarse_near, coarse_hop, coarse_smooth, coarse_shuffle,
    send_sem, recv_sem,
):
    nt, nz, cf, plane, cplane, cc, ncol, nta, ngz = sizes
    sites = nt * nz
    ta, gz, col = lax.axis_index("ta"), lax.axis_index("gz"), lax.axis_index("col")
    ring = nta * ncol
    here = ta * ncol + col
    after, before = lax.rem(here + 1, ring), lax.rem(here + ring - 1, ring)
    t_after = {"ta": after // ncol, "col": lax.rem(after, ncol)}
    t_before = {"ta": before // ncol, "col": lax.rem(before, ncol)}
    z_after = {"gz": lax.rem(gz + 1, ngz)}
    z_before = {"gz": lax.rem(gz + ngz - 1, ngz)}

    barrier = pltpu.get_barrier_semaphore()
    for device in (t_after, t_before, z_after, z_before):
        pl.semaphore_signal(barrier, inc=1, device_id=device, device_id_type=MESH)
    pl.semaphore_wait(barrier, 4)

    def exchange(buffer, number):
        inner_t, inner_z = pl.ds(1, nt), pl.ds(1, nz)
        plans = (
            (buffer.at[inner_t, 1], buffer.at[inner_t, nz + 1], z_before),
            (buffer.at[inner_t, nz], buffer.at[inner_t, 0], z_after),
            (buffer.at[1, inner_z], buffer.at[nt + 1, inner_z], t_before),
            (buffer.at[nt, inner_z], buffer.at[0, inner_z], t_after),
        )
        copies = []
        for index, (source, target, device) in enumerate(plans):
            copy = pltpu.make_async_remote_copy(
                src_ref=source,
                dst_ref=target,
                send_sem=send_sem.at[number, index],
                recv_sem=recv_sem.at[number, index],
                device_id=device,
                device_id_type=MESH,
            )
            copy.start()
            copies.append(copy)
        return copies

    def arrive(copies):
        for copy in copies:
            copy.wait_recv()

    def smooth(buffer):
        for t in range(nt):
            wide = jnp.concatenate([rest[t, z] for z in range(nz)], axis=1)
            wide = left_product(smooth_pair[...], wide)
            for z in range(nz):
                buffer[t + 1, z + 1] = wide[:, z * plane:(z + 1) * plane]

    def near(buffer):
        for t in range(nt):
            own = [buffer[t + 1, z + 1] for z in range(nz)]
            rows = jnp.concatenate([stacked(v, 1) for v in own], axis=0)
            moved = dot(rows, shuffle[...])
            terms = [jnp.concatenate(own, axis=1)]
            for k in range(4):
                terms.append(jnp.concatenate([
                    moved[z * cf:(z + 1) * cf, k * plane:(k + 1) * plane]
                    * weight_ref[4 + k, t, z:z + 1]
                    for z in range(nz)
                ], axis=1))
            image = left_product(near_pair[...], jnp.concatenate(terms, axis=0))
            for z in range(nz):
                rest[t, z] -= image[:, z * plane:(z + 1) * plane]

    def hops(buffer):
        for t in range(nt):
            terms = []
            for k, (dt, dz) in enumerate(((2, 1), (0, 1), (1, 2), (1, 0))):
                terms.append(jnp.concatenate([
                    buffer[t + dt, z + dz] * weight_ref[k, t, z:z + 1]
                    for z in range(nz)
                ], axis=1))
            image = left_product(hop_pair[...], jnp.concatenate(terms, axis=0))
            for z in range(nz):
                rest[t, z] -= image[:, z * plane:(z + 1) * plane]

    def add(buffer):
        for t in range(nt):
            for z in range(nz):
                solved[t, z] += buffer[t + 1, z + 1]

    pending = []
    smooth_pair[...] = stacked(smoother_ref[...], 0)
    for t in range(nt):
        for z in range(nz):
            rest[t, z] = rhs_ref[pl.ds(t * nz + z, cf, stride=sites), :]
    first = fields.at[0]
    smooth(first)
    copies = exchange(first, 0)
    pending += copies

    near_pair[...] = stacked(
        jnp.concatenate([blocks_ref[k] for k in (0, 5, 6, 7, 8)], axis=1), 0
    )
    hop_pair[...] = stacked(jnp.concatenate([blocks_ref[k] for k in (1, 2, 3, 4)], axis=1), 0)
    line = lax.broadcasted_iota(jnp.int32, (plane, plane), 0)
    for k in range(4):
        chosen = jnp.where(line == next_ref[k:k + 1, :], 1.0, 0.0).astype(BF16)
        shuffle[:, k * plane:(k + 1) * plane] = jnp.concatenate([chosen, chosen], axis=0)
    for t in range(nt):
        for z in range(nz):
            solved[t, z] = first[t + 1, z + 1]
    near(first)

    crows = sites * cplane
    line = lax.broadcasted_iota(jnp.int32, (crows, plane), 0)
    for s in range(sites):
        chosen = jnp.where(line == aggregate_ref[...] + s * cplane, 1.0, 0.0).astype(BF16)
        spread[:, s * plane:(s + 1) * plane] = jnp.concatenate([chosen, chosen], axis=0)
    restrict_pair[...] = stacked(restrict_ref[...], 1)
    prolong_pair[...] = stacked(jnp.transpose(prolong_ref[...]), 0)
    coarse_near[...] = stacked(
        jnp.concatenate([jnp.transpose(coarse_ref[k]) for k in (0, 5, 6, 7, 8)], axis=0), 1
    )
    coarse_hop[...] = stacked(
        jnp.concatenate([jnp.transpose(coarse_ref[k]) for k in (1, 2, 3, 4)], axis=0), 1
    )
    coarse_smooth[...] = stacked(jnp.transpose(coarse_smoother_ref[...]), 1)
    column = lax.broadcasted_iota(jnp.int32, (cplane, crows), 1)
    within = lax.rem(column, cplane)
    tiling = jnp.where(lax.broadcasted_iota(jnp.int32, (cplane, crows), 0) == within, 1.0, 0.0)
    padded_next = jnp.concatenate(
        [coarse_next_ref[...].astype(F32), jnp.zeros((4, cplane), F32)], axis=0
    )
    targets = dot(padded_next.astype(BF16), tiling.astype(BF16))
    line = lax.broadcasted_iota(jnp.int32, (crows, crows), 0).astype(F32)
    column = lax.broadcasted_iota(jnp.int32, (crows, crows), 1)
    start = (column - lax.rem(column, cplane)).astype(F32)
    for k, opposite in enumerate((1, 0, 3, 2)):
        chosen = jnp.where(line == start + targets[opposite:opposite + 1, :], 1.0, 0.0)
        chosen = chosen.astype(BF16)
        coarse_shuffle[k * crows:(k + 1) * crows, :] = jnp.concatenate([chosen, chosen], axis=1)

    arrive(copies)
    hops(first)

    second = fields.at[1]
    smooth(second)
    copies = exchange(second, 1)
    pending += copies
    near(second)
    add(second)
    arrive(copies)
    hops(second)

    line = lax.broadcasted_iota(jnp.int32, (2 * cplane, plane), 0)
    gather = jnp.where(line == aggregate_ref[...], 1.0, 0.0).astype(BF16)
    gather = jnp.concatenate([gather, gather], axis=1)
    sums = [
        dot(gather, stacked(rest[t, z], 1), NT)[:cplane]
        for t in range(nt) for z in range(nz)
    ]
    coarse_rhs[...] = right_product(jnp.concatenate(sums, axis=0), restrict_pair[...])

    def put(buffer, flat):
        for t in range(nt):
            for z in range(nz):
                s = t * nz + z
                buffer[t + 1, z + 1] = flat[s * cplane:(s + 1) * cplane]

    def shifted(buffer, dt, dz):
        return jnp.concatenate(
            [buffer[t + dt, z + dz] for t in range(nt) for z in range(nz)], axis=0
        )

    current = right_product(coarse_rhs[...], coarse_smooth[...])
    for sweep in range(SWEEPS):
        buffer = values.at[sweep]
        put(buffer, current)
        copies = exchange(buffer, 2 + POST + sweep)
        pending += copies
        moved = dot(coarse_shuffle[...], stacked(current, 0))
        terms = [current] + [moved[k * crows:(k + 1) * crows] for k in range(4)]
        rest_coarse = coarse_rhs[...] - right_product(
            jnp.concatenate(terms, axis=1), coarse_near[...]
        )
        arrive(copies)
        terms = [shifted(buffer, dt, dz) for dt, dz in ((2, 1), (0, 1), (1, 2), (1, 0))]
        rest_coarse -= right_product(jnp.concatenate(terms, axis=1), coarse_hop[...])
        current += right_product(rest_coarse, coarse_smooth[...])
    buffer = values.at[SWEEPS]
    put(buffer, current)
    copies = exchange(buffer, 2 + POST + SWEEPS)
    pending += copies

    correction = fields.at[2 + POST]

    def prolong(flat, places):
        lifted = stacked(left_product(prolong_pair[...], flat, NT), 1)
        rows = flat.shape[0]
        wide = dot(lifted, spread[...])
        for s, (t, z) in enumerate(places):
            correction[t, z] = wide[:, s * plane:(s + 1) * plane]

    prolong(current, [(t + 1, z + 1) for t in range(nt) for z in range(nz)])
    near(correction)
    add(correction)
    arrive(copies)
    around = [(nt + 1, z + 1) for z in range(nz)] + [(0, z + 1) for z in range(nz)]
    around += [(t + 1, nz + 1) for t in range(nt)] + [(t + 1, 0) for t in range(nt)]
    for begin in range(0, len(around), sites):
        places = around[begin:begin + sites]
        flat = [buffer[t, z] for t, z in places]
        flat += [jnp.zeros((cplane, cc), F32)] * (sites - len(places))
        prolong(jnp.concatenate(flat, axis=0), places)
    hops(correction)

    for sweep in range(POST):
        buffer = fields.at[2 + sweep]
        smooth(buffer)
        copies = exchange(buffer, 2 + sweep)
        pending += copies
        near(buffer)
        add(buffer)
        if sweep == POST - 1:
            for t in range(nt):
                for z in range(nz):
                    solution_ref[pl.ds(t * nz + z, cf, stride=sites), :] = solved[t, z]
        arrive(copies)
        hops(buffer)
    for t in range(nt):
        for z in range(nz):
            residual_ref[pl.ds(t * nz + z, cf, stride=sites), :] = rest[t, z]
    for copy in pending:
        copy.wait_send()


def solution(mesh):
    def shards(
        rhs_field, link_weights, fine_blocks, smoother, plane_next, aggregate,
        restrict_map, prolong_map, coarse_blocks, coarse_smoother, coarse_next,
    ):
        _, cf, nt, nz, plane = rhs_field.shape
        cplane = coarse_next.shape[1]
        cc = coarse_smoother.shape[0]
        sites = nt * nz
        crows = sites * cplane
        sizes = (
            nt, nz, cf, plane, cplane, cc,
            mesh.shape["col"], mesh.shape["ta"], mesh.shape["gz"],
        )
        exchanges = 3 + POST + SWEEPS
        out = jax.ShapeDtypeStruct((cf * sites, plane), F32)
        vmem = pl.BlockSpec(memory_space=pltpu.VMEM)
        solved, residual = pl.pallas_call(
            functools.partial(kernel, sizes),
            out_shape=(out, out),
            in_specs=[vmem] * 11,
            out_specs=(vmem, vmem),
            scratch_shapes=[
                pltpu.VMEM((3 + POST, nt + 2, nz + 2, cf, plane), F32),
                pltpu.VMEM((1 + SWEEPS, nt + 2, nz + 2, cplane, cc), F32),
                pltpu.VMEM((nt, nz, cf, plane), F32),
                pltpu.VMEM((nt, nz, cf, plane), F32),
                pltpu.VMEM((crows, cc), F32),
                pltpu.VMEM((2 * cf, 5 * cf), BF16),
                pltpu.VMEM((2 * cf, 4 * cf), BF16),
                pltpu.VMEM((2 * cf, cf), BF16),
                pltpu.VMEM((2 * plane, 4 * plane), BF16),
                pltpu.VMEM((2 * crows, sites * plane), BF16),
                pltpu.VMEM((cf, 2 * cc), BF16),
                pltpu.VMEM((2 * cf, cc), BF16),
                pltpu.VMEM((5 * cc, 2 * cc), BF16),
                pltpu.VMEM((4 * cc, 2 * cc), BF16),
                pltpu.VMEM((cc, 2 * cc), BF16),
                pltpu.VMEM((4 * crows, 2 * crows), BF16),
                pltpu.SemaphoreType.DMA((exchanges, 4)),
                pltpu.SemaphoreType.DMA((exchanges, 4)),
            ],
            compiler_params=pltpu.CompilerParams(
                collective_id=0, has_side_effects=True, vmem_limit_bytes=48 * 1024 * 1024
            ),
        )(
            rhs_field.reshape(cf * sites, plane), link_weights, fine_blocks, smoother,
            plane_next, aggregate.reshape(1, plane), restrict_map, prolong_map,
            coarse_blocks, coarse_smoother, coarse_next,
        )
        return solved.reshape(rhs_field.shape), residual.reshape(rhs_field.shape)

    return jax.shard_map(
        shards,
        mesh=mesh,
        in_specs=(
            P(None, None, ("ta", "col"), "gz", None),
            P(None, ("ta", "col"), "gz", None),
            P(), P(), P(), P(), P(), P(), P(), P(), P(),
        ),
        out_specs=(
            P(None, None, ("ta", "col"), "gz", None),
            P(None, None, ("ta", "col"), "gz", None),
        ),
        check_vma=False,
    )
```

profile of v0, /device:TPU:0, one launch (start us, length us, event | category | flops | bytes accessed | tf_op | source)
XLA Modules:
  0.0 77.6 jit_solution(15811928230576511482)
XLA Ops:
  0.6 0.0 copy-start.3
  0.6 0.0 copy-start.5
  0.7 0.0 copy-start.7
  0.7 0.0 copy-start.9
  0.7 0.9 %copy.13.prolong_ref = f32[128,96]{1,0:T(8,128)S(1)} copy(f32[128,96]{0,1:T(8,128)} %param.18) | data formatting | bytes 98304 | tf_op args[7]
  1.6 0.0 copy-done.3
  1.6 0.0 copy-done.5
  1.6 0.0 copy-done.7
  1.6 0.0 copy-done.9
  1.7 0.0 copy-start
  1.7 1.1 %copy-done = f32[1,96,4,4,128]{4,3,2,1,0:T(4,128)S(1)} copy-done((f32[1,96,4,4,128]{4,3,2,1,0:T(4,128)S(1)}, f32[1,96,4,4,128]{4,3,2,1,0:T(4,128)}, u32[]{:S(2)}) %copy-start) | copy-done | bytes 786456
  2.8 0.0 copy-start.1
  2.8 1.1 %copy-done.1 = f32[9,128,128]{2,1,0:T(8,128)S(1)} copy-done((f32[9,128,128]{2,1,0:T(8,128)S(1)}, f32[9,128,128]{2,1,0:T(8,128)}, u32[]{:S(2)}) %copy-start.1) | copy-done | bytes 589848
  3.9 0.0 copy-start.2
  3.9 1.0 %copy-done.2 = f32[9,96,96]{2,1,0:T(8,128)S(1)} copy-done((f32[9,96,96]{2,1,0:T(8,128)S(1)}, f32[9,96,96]{2,1,0:T(8,128)}, u32[]{:S(2)}) %copy-start.2) | copy-done | bytes 331800
  4.9 0.0 copy-start.4
  4.9 0.8 %copy-done.4 = f32[128,128]{1,0:T(8,128)S(1)} copy-done((f32[128,128]{1,0:T(8,128)S(1)}, f32[128,128]{1,0:T(8,128)}, u32[]{:S(2)}) %copy-start.4) | copy-done | bytes 65560
  5.7 0.0 copy-start.6
  5.7 0.8 %copy-done.6 = f32[96,128]{1,0:T(8,128)S(1)} copy-done((f32[96,128]{1,0:T(8,128)S(1)}, f32[96,128]{1,0:T(8,128)}, u32[]{:S(2)}) %copy-start.6) | copy-done | bytes 49176
  6.5 0.0 copy-start.8
  6.5 0.7 copy-done.8
  7.2 68.6 %shard_map.122 = (f32[1536,128]{1,0:T(8,128)S(1)}, f32[1536,128]{1,0:T(8,128)S(1)}) custom-call(f32[1536,128]{1,0:T(8,128)S(1)} %bitcast.4, f32[8,4,4,128]{3,2,1,0:T(4,128)S(1)} %copy-done.3, f32[9,96,96]{2,1,0:T(8,128)S(1)} %copy-done.2, f32[96,96]{1,0:T(8,128)S(1)} %copy-done.5, s32[4,128]{1,0:T(4,128)S(1)} %copy-done.7, s32[1,128]{1,0:T(1,128)S(1)} %bitcast.7, ...), custom_call_target="tpu_custom_call" | custom-call | tf_op jit(solution)/shard_map/pallas_call | solution.py:301
  75.8 0.9 %copy.16 = f32[1,96,4,4,128]{4,3,2,1,0:T(4,128)} copy(f32[1,96,4,4,128]{4,3,2,1,0:T(4,128)S(1)} %bitcast.6) | data formatting | bytes 1572864
  76.7 0.9 %copy.17 = f32[1,96,4,4,128]{4,3,2,1,0:T(4,128)} copy(f32[1,96,4,4,128]{4,3,2,1,0:T(4,128)S(1)} %bitcast.5) | data formatting | bytes 1572864
Async XLA Ops:
  0.6 1.0 %copy-start.3 = (f32[8,4,4,128]{3,2,1,0:T(4,128)S(1)}, f32[8,4,4,128]{3,2,1,0:T(4,128)}, u32[]{:S(2)}) copy-start(f32[8,4,4,128]{3,2,1,0:T(4,128)} %weight_ref.1) | copy-start | bytes 196612
  0.6 1.0 %copy-start.5 = (f32[96,96]{1,0:T(8,128)S(1)}, f32[96,96]{1,0:T(8,128)}, u32[]{:S(2)}) copy-start(f32[96,96]{1,0:T(8,128)} %smoother_ref.1) | copy-start | bytes 110596
  0.7 1.0 %copy-start.7 = (s32[4,128]{1,0:T(4,128)S(1)}, s32[4,128]{1,0:T(4,128)}, u32[]{:S(2)}) copy-start(s32[4,128]{1,0:T(4,128)} %next_ref.1) | copy-start | bytes 6148
  0.7 1.0 %copy-start.9 = (s32[128]{0:T(128)S(1)}, s32[128]{0:T(128)}, u32[]{:S(2)}) copy-start(s32[128]{0:T(128)} %param.16) | copy-start | bytes 1540
  1.7 1.1 %copy-start = (f32[1,96,4,4,128]{4,3,2,1,0:T(4,128)S(1)}, f32[1,96,4,4,128]{4,3,2,1,0:T(4,128)}, u32[]{:S(2)}) copy-start(f32[1,96,4,4,128]{4,3,2,1,0:T(4,128)} %param.11) | copy-start | bytes 2359300
  2.8 1.1 %copy-start.1 = (f32[9,128,128]{2,1,0:T(8,128)S(1)}, f32[9,128,128]{2,1,0:T(8,128)}, u32[]{:S(2)}) copy-start(f32[9,128,128]{2,1,0:T(8,128)} %coarse_ref.1) | copy-start | bytes 1769476
  3.9 1.0 %copy-start.2 = (f32[9,96,96]{2,1,0:T(8,128)S(1)}, f32[9,96,96]{2,1,0:T(8,128)}, u32[]{:S(2)}) copy-start(f32[9,96,96]{2,1,0:T(8,128)} %blocks_ref.1) | copy-start | bytes 995332
  4.9 0.8 %copy-start.4 = (f32[128,128]{1,0:T(8,128)S(1)}, f32[128,128]{1,0:T(8,128)}, u32[]{:S(2)}) copy-start(f32[128,128]{1,0:T(8,128)} %coarse_smoother_ref.1) | copy-start | bytes 196612
  5.7 0.8 %copy-start.6 = (f32[96,128]{1,0:T(8,128)S(1)}, f32[96,128]{1,0:T(8,128)}, u32[]{:S(2)}) copy-start(f32[96,128]{1,0:T(8,128)} %restrict_ref.1) | copy-start | bytes 147460
  6.5 0.7 copy-start.8
where the time goes:
time: 78 us; the launch traced here: 77.6 us
  Pallas kernels  68.6 us (88%)
  local copies, waits for them, and re-layouts  8.23 us (11%)
    pallas_call x1, Pallas kernels, shards(): pl.pallas_call(functools.partial(kernel, sizes), out_shape=(out, out), in...  68.6 us
    unnamed x23, local copies, waits for them, and re-layouts  8.23 us

commit v1 on v0

v1 whole, which is shorter than its diff:
```python
import functools

import jax
import jax.numpy as jnp
from jax import lax
from jax.experimental import pallas as pl
from jax.experimental.pallas import tpu as pltpu
from jax.sharding import PartitionSpec as P

SWEEPS = 3
F32 = jnp.float32
BF16 = jnp.bfloat16
MESH = pl.DeviceIdType.MESH
NN = (((1,), (0,)), ((), ()))
NT = (((1,), (1,)), ((), ()))


def dot(a, b, dims=NN):
    return lax.dot_general(a, b, dims, preferred_element_type=F32)


def split(x):
    hi = x.astype(BF16)
    return hi, (x - hi.astype(F32)).astype(BF16)


def stacked(x, axis):
    return jnp.concatenate(split(x), axis=axis)


def left_product(pair, x, dims=NN):
    rows = pair.shape[0] // 2
    hi, lo = split(x)
    both = dot(pair, hi, dims)
    return both[:rows] + both[rows:] + dot(pair[:rows], lo, dims)


def right_product(x, pair):
    columns = pair.shape[1] // 2
    hi, lo = split(x)
    both = dot(hi, pair)
    return both[:, :columns] + both[:, columns:] + dot(lo, pair[:, :columns])


def kernel(
    sizes,
    rhs_hbm, weight_hbm, blocks_hbm, smoother_hbm, next_hbm, aggregate_hbm,
    restrict_hbm, prolong_hbm, coarse_hbm, coarse_smoother_hbm, coarse_next_hbm,
    solution_ref, residual_ref,
    rhs_ref, weight_ref, blocks_ref, smoother_ref, next_ref, aggregate_ref,
    restrict_ref, prolong_ref, coarse_ref, coarse_smoother_ref, coarse_next_ref,
    fields, values, solved, rest, weights, coarse_rhs,
    near_pair, hop_pair, t_pair, z_pair, z_up_pair, z_down_pair, smooth_pair, shuffle, spread,
    restrict_pair, prolong_pair, coarse_near, coarse_hop, coarse_smooth, coarse_shuffle,
    load_sem, send_sem, recv_sem,
):
    nt, nz, cf, plane, cplane, cc, ncol, nta, ngz = sizes
    sites = nt * nz
    ta, gz, col = lax.axis_index("ta"), lax.axis_index("gz"), lax.axis_index("col")
    ring = nta * ncol
    here = ta * ncol + col
    after, before = lax.rem(here + 1, ring), lax.rem(here + ring - 1, ring)
    t_after = {"ta": after // ncol, "col": lax.rem(after, ncol)}
    t_before = {"ta": before // ncol, "col": lax.rem(before, ncol)}
    z_after = {"gz": lax.rem(gz + 1, ngz)}
    z_before = {"gz": lax.rem(gz + ngz - 1, ngz)}
    diagonals = [{**t_side, **z_side} for t_side in (t_before, t_after) for z_side in (z_before, z_after)]

    loads = {}
    for index, (name, source, target) in enumerate((
        ("rhs", rhs_hbm, rhs_ref), ("smoother", smoother_hbm, smoother_ref),
        ("weights", weight_hbm, weight_ref), ("blocks", blocks_hbm, blocks_ref),
        ("next", next_hbm, next_ref), ("aggregate", aggregate_hbm, aggregate_ref),
        ("restrict", restrict_hbm, restrict_ref), ("prolong", prolong_hbm, prolong_ref),
        ("coarse", coarse_hbm, coarse_ref),
        ("coarse_smoother", coarse_smoother_hbm, coarse_smoother_ref),
        ("coarse_next", coarse_next_hbm, coarse_next_ref),
    )):
        loads[name] = pltpu.make_async_copy(source, target, load_sem.at[index])
        loads[name].start()

    barrier = pltpu.get_barrier_semaphore()
    for device in [t_after, t_before, z_after, z_before] + diagonals:
        pl.semaphore_signal(barrier, inc=1, device_id=device, device_id_type=MESH)
    pl.semaphore_wait(barrier, 8)

    pending = []

    def send(number, index, source, target, device):
        copy = pltpu.make_async_remote_copy(
            src_ref=source,
            dst_ref=target,
            send_sem=send_sem.at[number, index],
            recv_sem=recv_sem.at[number, index],
            device_id=device,
            device_id_type=MESH,
        )
        copy.start()
        pending.append(copy)
        return copy

    def send_z(buffer, number, pad, width=1):
        inner = pl.ds(pad, nt)
        low, high = pl.ds(pad, width), pl.ds(pad + nz - width, width)
        above, below = pl.ds(pad + nz, width), pl.ds(pad - width, width)
        return [
            send(number, 0, buffer.at[inner, low], buffer.at[inner, above], z_before),
            send(number, 1, buffer.at[inner, high], buffer.at[inner, below], z_after),
        ]

    def send_t(buffer, number, pad, width=1):
        inner = pl.ds(pad, nz)
        low, high = pl.ds(pad, width), pl.ds(pad + nt - width, width)
        above, below = pl.ds(pad + nt, width), pl.ds(pad - width, width)
        return [
            send(number, 2, buffer.at[low, inner], buffer.at[above, inner], t_before),
            send(number, 3, buffer.at[high, inner], buffer.at[below, inner], t_after),
        ]

    def arrive(copies):
        for copy in copies:
            copy.wait_recv()

    rows = [[(t, z) for z in range(nz)] for t in range(nt)]
    columns = [[(t, z) for t in range(nt)] for z in range(nz)]
    edges_first = [0, nz - 1] + list(range(1, nz - 1))
    around = [
        [(-1, z) for z in range(nz)], [(nt, z) for z in range(nz)],
        [(t, -1) for t in range(nt)], [(t, nz) for t in range(nt)],
    ]
    t_hops = ((0, 1, 0), (1, -1, 0))
    z_hops = ((2, 0, 1), (3, 0, -1))

    def lanes(x, s):
        return x[:, s * plane:(s + 1) * plane]

    def take(image, places):
        for s, (t, z) in enumerate(places):
            rest[t + 1, z + 1] -= lanes(image, s)

    def smooth(buffer, places):
        wide = jnp.concatenate([rest[t + 1, z + 1] for t, z in places], axis=1)
        wide = left_product(smooth_pair[...], wide)
        for s, (t, z) in enumerate(places):
            buffer[t + 2, z + 2] = lanes(wide, s)

    def near(buffer, places):
        own = [buffer[t + 2, z + 2] for t, z in places]
        moved = dot(jnp.concatenate([stacked(v, 1) for v in own], axis=0), shuffle[...])
        terms = [jnp.concatenate(own, axis=1)]
        for k in range(4):
            terms.append(jnp.concatenate([
                moved[s * cf:(s + 1) * cf, k * plane:(k + 1) * plane]
                * weights[t + 1, z + 1, 4 + k:5 + k]
                for s, (t, z) in enumerate(places)
            ], axis=1))
        take(left_product(near_pair[...], jnp.concatenate(terms, axis=0)), places)

    def hops(buffer, places, pair, shifts):
        terms = [
            jnp.concatenate([
                buffer[t + 2 + dt, z + 2 + dz] * weights[t + 1, z + 1, k:k + 1]
                for t, z in places
            ], axis=1)
            for k, dt, dz in shifts
        ]
        take(left_product(pair[...], jnp.concatenate(terms, axis=0)), places)

    def inner_z(buffer):
        hops(buffer, columns[0], z_up_pair, z_hops[:1])
        hops(buffer, columns[-1], z_down_pair, z_hops[1:])
        for places in columns[1:-1]:
            hops(buffer, places, z_pair, z_hops)

    def outer_z(buffer, z):
        if z == 0:
            hops(buffer, columns[0], z_down_pair, z_hops[1:])
        if z == nz - 1:
            hops(buffer, columns[-1], z_up_pair, z_hops[:1])

    def add(buffer):
        for t in range(nt):
            for z in range(nz):
                solved[t, z] += buffer[t + 2, z + 2]

    loads["rhs"].wait()
    loads["smoother"].wait()
    smooth_pair[...] = stacked(smoother_ref[...], 0)
    first = fields.at[0]
    for z in edges_first:
        for t in range(nt):
            rest[t + 1, z + 1] = rhs_ref[pl.ds(t * nz + z, cf, stride=sites), :]
        smooth(first, columns[z])
        if z == nz - 1:
            z_copies = send_z(first, 0, 2)
    t_copies = send_t(first, 0, 2)

    for name in ("weights", "blocks", "next"):
        loads[name].wait()
    for t in range(nt):
        for z in range(nz):
            weights[t + 1, z + 1] = weight_ref[pl.ds(t * nz + z, 8, stride=sites), :]
    weight_copies = send_z(weights, 4, 1) + send_t(weights, 4, 1)
    blocks = [blocks_ref[k] for k in range(9)]
    near_pair[...] = stacked(jnp.concatenate([blocks[k] for k in (0, 5, 6, 7, 8)], axis=1), 0)
    hop_pair[...] = stacked(jnp.concatenate(blocks[1:5], axis=1), 0)
    t_pair[...] = stacked(jnp.concatenate(blocks[1:3], axis=1), 0)
    z_pair[...] = stacked(jnp.concatenate(blocks[3:5], axis=1), 0)
    z_up_pair[...] = stacked(blocks[3], 0)
    z_down_pair[...] = stacked(blocks[4], 0)
    line = lax.broadcasted_iota(jnp.int32, (plane, plane), 0)
    for k in range(4):
        chosen = jnp.where(line == next_ref[k:k + 1, :], 1.0, 0.0).astype(BF16)
        shuffle[:, k * plane:(k + 1) * plane] = jnp.concatenate([chosen, chosen], axis=0)
    for t in range(nt):
        for z in range(nz):
            solved[t, z] = first[t + 2, z + 2]
    for places in rows:
        near(first, places)
    inner_z(first)

    for name in (
        "aggregate", "restrict", "prolong", "coarse", "coarse_smoother", "coarse_next"
    ):
        loads[name].wait()
    crows = sites * cplane
    line = lax.broadcasted_iota(jnp.int32, (crows, plane), 0)
    for s in range(sites):
        chosen = jnp.where(line == aggregate_ref[...] + s * cplane, 1.0, 0.0).astype(BF16)
        spread[:, s * plane:(s + 1) * plane] = jnp.concatenate([chosen, chosen], axis=0)
    restrict_pair[...] = stacked(restrict_ref[...], 1)
    prolong_pair[...] = stacked(prolong_ref[...], 0)
    coarse_near[...] = stacked(
        jnp.concatenate([jnp.transpose(coarse_ref[k]) for k in (0, 5, 6, 7, 8)], axis=0), 1
    )
    coarse_hop[...] = stacked(
        jnp.concatenate([jnp.transpose(coarse_ref[k]) for k in (1, 2, 3, 4)], axis=0), 1
    )
    coarse_smooth[...] = stacked(jnp.transpose(coarse_smoother_ref[...]), 1)
    column = lax.broadcasted_iota(jnp.int32, (cplane, crows), 1)
    within = lax.rem(column, cplane)
    tiling = jnp.where(lax.broadcasted_iota(jnp.int32, (cplane, crows), 0) == within, 1.0, 0.0)
    padded_next = jnp.concatenate(
        [coarse_next_ref[...].astype(F32), jnp.zeros((4, cplane), F32)], axis=0
    )
    targets = dot(padded_next.astype(BF16), tiling.astype(BF16))
    line = lax.broadcasted_iota(jnp.int32, (crows, crows), 0).astype(F32)
    column = lax.broadcasted_iota(jnp.int32, (crows, crows), 1)
    start = (column - lax.rem(column, cplane)).astype(F32)
    for k, opposite in enumerate((1, 0, 3, 2)):
        chosen = jnp.where(line == start + targets[opposite:opposite + 1, :], 1.0, 0.0)
        chosen = chosen.astype(BF16)
        coarse_shuffle[k * crows:(k + 1) * crows, :] = jnp.concatenate([chosen, chosen], axis=1)

    arrive(t_copies)
    for places in rows:
        hops(first, places, t_pair, t_hops)
    arrive(z_copies)

    second = fields.at[1]
    for z in edges_first:
        outer_z(first, z)
        smooth(second, columns[z])
        if z == nz - 1:
            z_copies = send_z(second, 1, 2)
    t_copies = send_t(second, 1, 2)
    for places in rows:
        near(second, places)
    inner_z(second)
    add(second)
    arrive(t_copies)
    for places in rows:
        hops(second, places, t_pair, t_hops)
    arrive(z_copies)
    outer_z(second, 0)
    outer_z(second, nz - 1)

    rest_copies = send_z(rest, 2, 1) + send_t(rest, 2, 1)

    line = lax.broadcasted_iota(jnp.int32, (2 * cplane, plane), 0)
    gather = jnp.where(line == aggregate_ref[...], 1.0, 0.0).astype(BF16)
    gather = jnp.concatenate([gather, gather], axis=1)
    sums = [
        dot(gather, stacked(rest[t + 1, z + 1], 1), NT)[:cplane]
        for t in range(nt) for z in range(nz)
    ]
    coarse_rhs[...] = right_product(jnp.concatenate(sums, axis=0), restrict_pair[...])

    def put(buffer, flat):
        for t in range(nt):
            for z in range(nz):
                s = t * nz + z
                buffer[t + 2, z + 2] = flat[s * cplane:(s + 1) * cplane]

    def shifted(buffer, dt, dz):
        return jnp.concatenate(
            [buffer[t + 2 + dt, z + 2 + dz] for t in range(nt) for z in range(nz)], axis=0
        )

    current = right_product(coarse_rhs[...], coarse_smooth[...])
    for sweep in range(SWEEPS):
        buffer = values.at[sweep]
        put(buffer, current)
        copies = send_z(buffer, 5 + sweep, 2) + send_t(buffer, 5 + sweep, 2)
        moved = dot(coarse_shuffle[...], stacked(current, 0))
        terms = [current] + [moved[k * crows:(k + 1) * crows] for k in range(4)]
        rest_coarse = coarse_rhs[...] - right_product(
            jnp.concatenate(terms, axis=1), coarse_near[...]
        )
        arrive(copies)
        terms = [shifted(buffer, dt, dz) for _, dt, dz in t_hops + z_hops]
        rest_coarse -= right_product(jnp.concatenate(terms, axis=1), coarse_hop[...])
        current += right_product(rest_coarse, coarse_smooth[...])
    buffer = values.at[SWEEPS]
    put(buffer, current)
    number = 5 + SWEEPS
    copies = send_z(buffer, number, 2, 2) + send_t(buffer, number, 2, 2)
    sides = [(t, z) for t in (0, 1) for z in (0, 1)]
    for index, (device, (t, z)) in enumerate(zip(diagonals, sides)):
        source = buffer.at[1 + nt if t else 2, 1 + nz if z else 2]
        target = buffer.at[1 if t else 2 + nt, 1 if z else 2 + nz]
        copies.append(send(number, 4 + index, source, target, device))

    correction = fields.at[2]

    def prolong(flat, places):
        lifted = stacked(left_product(prolong_pair[...], flat, NT), 1)
        wide = dot(lifted, spread[...])
        for s, (t, z) in enumerate(places):
            correction[t + 2, z + 2] = lanes(wide, s)

    prolong(current, [place for places in rows for place in places])
    for copy in rest_copies:
        copy.wait_send()
    pending[:] = [copy for copy in pending if not any(copy is done for done in rest_copies)]
    for places in rows:
        near(correction, places)
    inner_z(correction)
    add(correction)
    arrive(copies)
    halo = [place for places in around for place in places]
    halo += [(t, z) for t in (-2, nt + 1) for z in range(nz)]
    halo += [(t, z) for t in range(nt) for z in (-2, nz + 1)]
    halo += [(t, z) for t in (-1, nt) for z in (-1, nz)]
    for begin in range(0, len(halo), sites):
        places = halo[begin:begin + sites]
        flat = [buffer[t + 2, z + 2] for t, z in places]
        flat += [jnp.zeros((cplane, cc), F32)] * (sites - len(places))
        prolong(jnp.concatenate(flat, axis=0), places)
    for places in rows:
        hops(correction, places, t_pair, t_hops)
    outer_z(correction, 0)
    outer_z(correction, nz - 1)
    arrive(weight_copies)
    arrive(rest_copies)
    third = fields.at[3]
    for places in around:
        near(correction, places)
        hops(correction, places, hop_pair, t_hops + z_hops)
        smooth(third, places)
    for places in columns:
        smooth(third, places)

    last = fields.at[4]
    for z in edges_first:
        near(third, columns[z])
        hops(third, columns[z], hop_pair, t_hops + z_hops)
        smooth(last, columns[z])
        if z == nz - 1:
            z_copies = send_z(last, 3, 2)
    t_copies = send_t(last, 3, 2)
    for t in range(nt):
        for z in range(nz):
            solution_ref[pl.ds(t * nz + z, cf, stride=sites), :] = (
                solved[t, z] + third[t + 2, z + 2] + last[t + 2, z + 2]
            )
    for places in rows:
        near(last, places)
    inner_z(last)
    arrive(t_copies)
    for places in rows:
        hops(last, places, t_pair, t_hops)
    for places in columns[1:-1]:
        for t, z in places:
            residual_ref[pl.ds(t * nz + z, cf, stride=sites), :] = rest[t + 1, z + 1]
    arrive(z_copies)
    for places in (columns[0], columns[-1]):
        outer_z(last, places[0][1])
        for t, z in places:
            residual_ref[pl.ds(t * nz + z, cf, stride=sites), :] = rest[t + 1, z + 1]
    for copy in pending:
        copy.wait_send()


def solution(mesh):
    def shards(
        rhs_field, link_weights, fine_blocks, smoother, plane_next, aggregate,
        restrict_map, prolong_map, coarse_blocks, coarse_smoother, coarse_next,
    ):
        _, cf, nt, nz, plane = rhs_field.shape
        cplane = coarse_next.shape[1]
        cc = coarse_smoother.shape[0]
        sites = nt * nz
        crows = sites * cplane
        sizes = (
            nt, nz, cf, plane, cplane, cc,
            mesh.shape["col"], mesh.shape["ta"], mesh.shape["gz"],
        )
        out = jax.ShapeDtypeStruct((cf * sites, plane), F32)
        vmem = pl.BlockSpec(memory_space=pltpu.VMEM)
        hbm = pl.BlockSpec(memory_space=pltpu.HBM)
        operands = (
            rhs_field.reshape(cf * sites, plane), link_weights.reshape(-1, plane), fine_blocks,
            smoother, plane_next, aggregate.reshape(1, plane), restrict_map, prolong_map.T,
            coarse_blocks, coarse_smoother, coarse_next,
        )
        solved, residual = pl.pallas_call(
            functools.partial(kernel, sizes),
            out_shape=(out, out),
            in_specs=[hbm] * len(operands),
            out_specs=(vmem, vmem),
            scratch_shapes=[pltpu.VMEM(operand.shape, operand.dtype) for operand in operands] + [
                pltpu.VMEM((5, nt + 4, nz + 4, cf, plane), F32),
                pltpu.VMEM((1 + SWEEPS, nt + 4, nz + 4, cplane, cc), F32),
                pltpu.VMEM((nt, nz, cf, plane), F32),
                pltpu.VMEM((nt + 2, nz + 2, cf, plane), F32),
                pltpu.VMEM((nt + 2, nz + 2, 8, plane), F32),
                pltpu.VMEM((crows, cc), F32),
                pltpu.VMEM((2 * cf, 5 * cf), BF16),
                pltpu.VMEM((2 * cf, 4 * cf), BF16),
                pltpu.VMEM((2 * cf, 2 * cf), BF16),
                pltpu.VMEM((2 * cf, 2 * cf), BF16),
                pltpu.VMEM((2 * cf, cf), BF16),
                pltpu.VMEM((2 * cf, cf), BF16),
                pltpu.VMEM((2 * cf, cf), BF16),
                pltpu.VMEM((2 * plane, 4 * plane), BF16),
                pltpu.VMEM((2 * crows, sites * plane), BF16),
                pltpu.VMEM((cf, 2 * cc), BF16),
                pltpu.VMEM((2 * cf, cc), BF16),
                pltpu.VMEM((5 * cc, 2 * cc), BF16),
                pltpu.VMEM((4 * cc, 2 * cc), BF16),
                pltpu.VMEM((cc, 2 * cc), BF16),
                pltpu.VMEM((4 * crows, 2 * crows), BF16),
                pltpu.SemaphoreType.DMA((len(operands),)),
                pltpu.SemaphoreType.DMA((6 + SWEEPS, 8)),
                pltpu.SemaphoreType.DMA((6 + SWEEPS, 8)),
            ],
            compiler_params=pltpu.CompilerParams(
                collective_id=0, has_side_effects=True, vmem_limit_bytes=63 * 1024 * 1024
            ),
        )(*operands)
        return solved.reshape(rhs_field.shape), residual.reshape(rhs_field.shape)

    return jax.shard_map(
        shards,
        mesh=mesh,
        in_specs=(
            P(None, None, ("ta", "col"), "gz", None),
            P(None, ("ta", "col"), "gz", None),
            P(), P(), P(), P(), P(), P(), P(), P(), P(),
        ),
        out_specs=(
            P(None, None, ("ta", "col"), "gz", None),
            P(None, None, ("ta", "col"), "gz", None),
        ),
        check_vma=False,
    )
```

time: 78 us -> 77.4 us (level)
  local copies, waits for them, and re-layouts: 8.23 us -> 3.02 us
  Pallas kernels: 68.6 us -> 73.6 us
    unnamed x23 -> x4, local copies, waits for them, and re-layouts: 8.23 us -> 3.02 us
    pallas_call x1, Pallas kernels: 68.6 us -> 73.6 us  [shards(): pl.pallas_call(functools.partial(kernel, sizes), out_shape=(out, out), in...]
where the time goes in v1:
time: 77.4 us; the launch traced here: 77.2 us
  Pallas kernels  73.6 us (95%)
  local copies, waits for them, and re-layouts  3.02 us (4%)
    pallas_call x1, Pallas kernels, shards(): pl.pallas_call(functools.partial(kernel, sizes), out_shape=(out, out), in...  73.6 us
    unnamed x4, local copies, waits for them, and re-layouts  3.02 us

profile of v1, /device:TPU:0, one launch (start us, length us, event | category | flops | bytes accessed | tf_op | source)
XLA Modules:
  0.0 77.2 jit_solution(4469225158972019191)
XLA Ops:
  0.6 73.6 %shard_map.122 = (f32[1536,128]{1,0:T(8,128)}, f32[1536,128]{1,0:T(8,128)}) custom-call(f32[1536,128]{1,0:T(8,128)} %bitcast.6, f32[128,128]{1,0:T(8,128)} %bitcast.9, f32[9,96,96]{2,1,0:T(8,128)} %blocks_hbm.1, f32[96,96]{1,0:T(8,128)} %smoother_hbm.1, s32[4,128]{1,0:T(4,128)} %next_hbm.1, s32[1,128]{1,0:T(1,128)} %bitcast.11, f32[96,128]{1,0:T(8,128)} %restrict_hbm.1, ...), custom_call_target="tpu_custom_call" | custom-call | tf_op jit(solution)/shard_map/pallas_call | solution.py:417
  74.2 0.0 copy-start
  74.2 2.1 %copy.15 = f32[1,96,4,4,128]{4,3,2,1,0:T(4,128)} copy(f32[1,96,4,4,128]{4,3,2,1,0:T(4,128)} %bitcast.8) | data formatting | bytes 1572864
  76.4 0.0 copy-done
  76.4 0.9 %copy.16 = f32[1,96,4,4,128]{4,3,2,1,0:T(4,128)} copy(f32[1,96,4,4,128]{4,3,2,1,0:T(4,128)S(1)} %bitcast.7) | data formatting | bytes 1572864
Async XLA Ops:
  74.2 2.1 %copy-start = (f32[1536,128]{1,0:T(8,128)S(1)}, f32[1536,128]{1,0:T(8,128)}, u32[]{:S(2)}) copy-start(f32[1536,128]{1,0:T(8,128)} %get-tuple-element.5) | copy-start | bytes 2359300

commit v2 on v1

--- a/solution.py
+++ b/solution.py
@@ -49,8 +49,8 @@
     solution_ref, residual_ref,
     rhs_ref, weight_ref, blocks_ref, smoother_ref, next_ref, aggregate_ref,
     restrict_ref, prolong_ref, coarse_ref, coarse_smoother_ref, coarse_next_ref,
-    fields, values, solved, rest, weights, coarse_rhs,
-    near_pair, hop_pair, t_pair, z_pair, z_up_pair, z_down_pair, smooth_pair, shuffle, spread,
+    fields, values, weights, coarse_rhs,
+    all_pairs, down_pairs, single_pairs, smooth_pair, shuffle, spread,
     restrict_pair, prolong_pair, coarse_near, coarse_hop, coarse_smooth, coarse_shuffle,
     load_sem, send_sem, recv_sem,
 ):
@@ -128,96 +128,100 @@
         [(-1, z) for z in range(nz)], [(nt, z) for z in range(nz)],
         [(t, -1) for t in range(nt)], [(t, nz) for t in range(nt)],
     ]
-    t_hops = ((0, 1, 0), (1, -1, 0))
-    z_hops = ((2, 0, 1), (3, 0, -1))
+    steps = {1: (1, 0), 2: (-1, 0), 3: (0, 1), 4: (0, -1)}
+    order = (0, 5, 6, 7, 8, 3, 4, 1, 2)
+    down_order = order[:7] + (2,)
 
     def lanes(x, s):
         return x[:, s * plane:(s + 1) * plane]
 
-    def take(image, places):
+    def image(source, places, pair, terms, local):
+        own = [source[t + 2, z + 2] for t, z in places]
+        if 5 in terms:
+            moved = dot(jnp.concatenate([stacked(v, 1) for v in own], axis=0), shuffle[...])
+        parts = []
+        for k in terms:
+            if k == 0:
+                row = own
+            elif k > 4:
+                row = [
+                    moved[s * cf:(s + 1) * cf, (k - 5) * plane:(k - 4) * plane]
+                    * weights[t + 1, z + 1, k - 1:k]
+                    for s, (t, z) in enumerate(places)
+                ]
+            else:
+                dt, dz = steps[k]
+                row = [
+                    jnp.zeros((cf, plane), F32)
+                    if local and not (0 <= t + dt < nt and 0 <= z + dz < nz)
+                    else source[t + 2 + dt, z + 2 + dz] * weights[t + 1, z + 1, k - 1:k]
+                    for t, z in places
+                ]
+            parts.append(jnp.concatenate(row, axis=1))
+        wide = parts[0] if len(parts) == 1 else jnp.concatenate(parts, axis=0)
+        return left_product(pair[...], wide)
+
+    def less(base, target, places, wide):
         for s, (t, z) in enumerate(places):
-            rest[t + 1, z + 1] -= lanes(image, s)
-
-    def smooth(buffer, places):
-        wide = jnp.concatenate([rest[t + 1, z + 1] for t, z in places], axis=1)
-        wide = left_product(smooth_pair[...], wide)
-        for s, (t, z) in enumerate(places):
-            buffer[t + 2, z + 2] = lanes(wide, s)
-
-    def near(buffer, places):
-        own = [buffer[t + 2, z + 2] for t, z in places]
-        moved = dot(jnp.concatenate([stacked(v, 1) for v in own], axis=0), shuffle[...])
-        terms = [jnp.concatenate(own, axis=1)]
-        for k in range(4):
-            terms.append(jnp.concatenate([
-                moved[s * cf:(s + 1) * cf, k * plane:(k + 1) * plane]
-                * weights[t + 1, z + 1, 4 + k:5 + k]
-                for s, (t, z) in enumerate(places)
-            ], axis=1))
-        take(left_product(near_pair[...], jnp.concatenate(terms, axis=0)), places)
-
-    def hops(buffer, places, pair, shifts):
-        terms = [
-            jnp.concatenate([
-                buffer[t + 2 + dt, z + 2 + dz] * weights[t + 1, z + 1, k:k + 1]
-                for t, z in places
-            ], axis=1)
-            for k, dt, dz in shifts
-        ]
-        take(left_product(pair[...], jnp.concatenate(terms, axis=0)), places)
-
-    def inner_z(buffer):
-        hops(buffer, columns[0], z_up_pair, z_hops[:1])
-        hops(buffer, columns[-1], z_down_pair, z_hops[1:])
-        for places in columns[1:-1]:
-            hops(buffer, places, z_pair, z_hops)
-
-    def outer_z(buffer, z):
-        if z == 0:
-            hops(buffer, columns[0], z_down_pair, z_hops[1:])
-        if z == nz - 1:
-            hops(buffer, columns[-1], z_up_pair, z_hops[:1])
-
-    def add(buffer):
-        for t in range(nt):
-            for z in range(nz):
-                solved[t, z] += buffer[t + 2, z + 2]
-
+            target[t + 2, z + 2] = base[t + 2, z + 2] - lanes(wide, s)
+
+    def local_terms(form, source, base, target):
+        for t, places in enumerate(rows):
+            if t == 0:
+                pair, terms = all_pairs.at[form, :, pl.ds(0, 8 * cf)], order[:8]
+            elif t == nt - 1:
+                pair, terms = down_pairs.at[form], down_order
+            else:
+                pair, terms = all_pairs.at[form], order
+            less(base, target, places, image(source, places, pair, terms, True))
+
+    def edge(form, source, target, k, places):
+        wide = image(source, places, single_pairs.at[form, k - 1], (k,), False)
+        less(target, target, places, wide)
+
+    def t_edges(form, source, target):
+        edge(form, source, target, 1, rows[-1])
+        edge(form, source, target, 2, rows[0])
+
+    def z_edges(form, source, target):
+        edge(form, source, target, 4, columns[0])
+        edge(form, source, target, 3, columns[-1])
+
+    def all_terms(form, source, base, target, places):
+        less(base, target, places, image(source, places, all_pairs.at[form], order, False))
+
+    r0, r1, r2, r3, r4, r5, correction = [fields.at[index] for index in range(7)]
     loads["rhs"].wait()
-    loads["smoother"].wait()
-    smooth_pair[...] = stacked(smoother_ref[...], 0)
-    first = fields.at[0]
     for z in edges_first:
         for t in range(nt):
-            rest[t + 1, z + 1] = rhs_ref[pl.ds(t * nz + z, cf, stride=sites), :]
-        smooth(first, columns[z])
+            r0[t + 2, z + 2] = rhs_ref[pl.ds(t * nz + z, cf, stride=sites), :]
         if z == nz - 1:
-            z_copies = send_z(first, 0, 2)
-    t_copies = send_t(first, 0, 2)
-
-    for name in ("weights", "blocks", "next"):
+            z_copies = send_z(r0, 0, 2)
+    t_copies = send_t(r0, 0, 2)
+
+    for name in ("smoother", "weights", "blocks", "next"):
         loads[name].wait()
     for t in range(nt):
         for z in range(nz):
             weights[t + 1, z + 1] = weight_ref[pl.ds(t * nz + z, 8, stride=sites), :]
     weight_copies = send_z(weights, 4, 1) + send_t(weights, 4, 1)
+    smooth_pair[...] = stacked(smoother_ref[...], 0)
     blocks = [blocks_ref[k] for k in range(9)]
-    near_pair[...] = stacked(jnp.concatenate([blocks[k] for k in (0, 5, 6, 7, 8)], axis=1), 0)
-    hop_pair[...] = stacked(jnp.concatenate(blocks[1:5], axis=1), 0)
-    t_pair[...] = stacked(jnp.concatenate(blocks[1:3], axis=1), 0)
-    z_pair[...] = stacked(jnp.concatenate(blocks[3:5], axis=1), 0)
-    z_up_pair[...] = stacked(blocks[3], 0)
-    z_down_pair[...] = stacked(blocks[4], 0)
+    smoothed = lax.dot_general(
+        jnp.concatenate(blocks, axis=0), smoother_ref[...], NN,
+        precision=lax.Precision.HIGHEST, preferred_element_type=F32,
+    )
+    smoothed = [smoothed[k * cf:(k + 1) * cf] for k in range(9)]
+    for form, parts in enumerate((smoothed, blocks)):
+        all_pairs[form] = stacked(jnp.concatenate([parts[k] for k in order], axis=1), 0)
+        down_pairs[form] = stacked(jnp.concatenate([parts[k] for k in down_order], axis=1), 0)
+        for k in range(1, 5):
+            single_pairs[form, k - 1] = stacked(parts[k], 0)
     line = lax.broadcasted_iota(jnp.int32, (plane, plane), 0)
     for k in range(4):
         chosen = jnp.where(line == next_ref[k:k + 1, :], 1.0, 0.0).astype(BF16)
         shuffle[:, k * plane:(k + 1) * plane] = jnp.concatenate([chosen, chosen], axis=0)
-    for t in range(nt):
-        for z in range(nz):
-            solved[t, z] = first[t + 2, z + 2]
-    for places in rows:
-        near(first, places)
-    inner_z(first)
+    local_terms(0, r0, r0, r1)
 
     for name in (
         "aggregate", "restrict", "prolong", "coarse", "coarse_smoother", "coarse_next"
@@ -253,35 +257,24 @@
         coarse_shuffle[k * crows:(k + 1) * crows, :] = jnp.concatenate([chosen, chosen], axis=1)
 
     arrive(t_copies)
-    for places in rows:
-        hops(first, places, t_pair, t_hops)
+    t_edges(0, r0, r1)
     arrive(z_copies)
-
-    second = fields.at[1]
-    for z in edges_first:
-        outer_z(first, z)
-        smooth(second, columns[z])
-        if z == nz - 1:
-            z_copies = send_z(second, 1, 2)
-    t_copies = send_t(second, 1, 2)
-    for places in rows:
-        near(second, places)
-    inner_z(second)
-    add(second)
+    z_edges(0, r0, r1)
+    z_copies = send_z(r1, 1, 2)
+    t_copies = send_t(r1, 1, 2)
+    local_terms(0, r1, r1, r2)
     arrive(t_copies)
-    for places in rows:
-        hops(second, places, t_pair, t_hops)
+    t_edges(0, r1, r2)
     arrive(z_copies)
-    outer_z(second, 0)
-    outer_z(second, nz - 1)
-
-    rest_copies = send_z(rest, 2, 1) + send_t(rest, 2, 1)
+    z_edges(0, r1, r2)
+
+    rest_copies = send_z(r2, 2, 2) + send_t(r2, 2, 2)
 
     line = lax.broadcasted_iota(jnp.int32, (2 * cplane, plane), 0)
     gather = jnp.where(line == aggregate_ref[...], 1.0, 0.0).astype(BF16)
     gather = jnp.concatenate([gather, gather], axis=1)
     sums = [
-        dot(gather, stacked(rest[t + 1, z + 1], 1), NT)[:cplane]
+        dot(gather, stacked(r2[t + 2, z + 2], 1), NT)[:cplane]
         for t in range(nt) for z in range(nz)
     ]
     coarse_rhs[...] = right_product(jnp.concatenate(sums, axis=0), restrict_pair[...])
@@ -308,7 +301,7 @@
             jnp.concatenate(terms, axis=1), coarse_near[...]
         )
         arrive(copies)
-        terms = [shifted(buffer, dt, dz) for _, dt, dz in t_hops + z_hops]
+        terms = [shifted(buffer, dt, dz) for dt, dz in steps.values()]
         rest_coarse -= right_product(jnp.concatenate(terms, axis=1), coarse_hop[...])
         current += right_product(rest_coarse, coarse_smooth[...])
     buffer = values.at[SWEEPS]
@@ -321,8 +314,6 @@
         target = buffer.at[1 if t else 2 + nt, 1 if z else 2 + nz]
         copies.append(send(number, 4 + index, source, target, device))
 
-    correction = fields.at[2]
-
     def prolong(flat, places):
         lifted = stacked(left_product(prolong_pair[...], flat, NT), 1)
         wide = dot(lifted, spread[...])
@@ -330,13 +321,7 @@
             correction[t + 2, z + 2] = lanes(wide, s)
 
     prolong(current, [place for places in rows for place in places])
-    for copy in rest_copies:
-        copy.wait_send()
-    pending[:] = [copy for copy in pending if not any(copy is done for done in rest_copies)]
-    for places in rows:
-        near(correction, places)
-    inner_z(correction)
-    add(correction)
+    local_terms(1, correction, r2, r3)
     arrive(copies)
     halo = [place for places in around for place in places]
     halo += [(t, z) for t in (-2, nt + 1) for z in range(nz)]
@@ -347,47 +332,39 @@
         flat = [buffer[t + 2, z + 2] for t, z in places]
         flat += [jnp.zeros((cplane, cc), F32)] * (sites - len(places))
         prolong(jnp.concatenate(flat, axis=0), places)
-    for places in rows:
-        hops(correction, places, t_pair, t_hops)
-    outer_z(correction, 0)
-    outer_z(correction, nz - 1)
+    t_edges(1, correction, r3)
+    z_edges(1, correction, r3)
     arrive(weight_copies)
     arrive(rest_copies)
-    third = fields.at[3]
     for places in around:
-        near(correction, places)
-        hops(correction, places, hop_pair, t_hops + z_hops)
-        smooth(third, places)
-    for places in columns:
-        smooth(third, places)
-
-    last = fields.at[4]
+        all_terms(1, correction, r2, r3, places)
+
     for z in edges_first:
-        near(third, columns[z])
-        hops(third, columns[z], hop_pair, t_hops + z_hops)
-        smooth(last, columns[z])
+        all_terms(0, r3, r3, r4, columns[z])
         if z == nz - 1:
-            z_copies = send_z(last, 3, 2)
-    t_copies = send_t(last, 3, 2)
-    for t in range(nt):
-        for z in range(nz):
+            z_copies = send_z(r4, 3, 2)
+    t_copies = send_t(r4, 3, 2)
+    local_terms(0, r4, r4, r5)
+    for places in rows:
+        wide = jnp.concatenate([
+            r0[t + 2, z + 2] + r1[t + 2, z + 2] + r3[t + 2, z + 2] + r4[t + 2, z + 2]
+            for t, z in places
+        ], axis=1)
+        wide = left_product(smooth_pair[...], wide)
+        for s, (t, z) in enumerate(places):
             solution_ref[pl.ds(t * nz + z, cf, stride=sites), :] = (
-                solved[t, z] + third[t + 2, z + 2] + last[t + 2, z + 2]
+                correction[t + 2, z + 2] + lanes(wide, s)
             )
-    for places in rows:
-        near(last, places)
-    inner_z(last)
     arrive(t_copies)
-    for places in rows:
-        hops(last, places, t_pair, t_hops)
+    t_edges(0, r4, r5)
     for places in columns[1:-1]:
         for t, z in places:
-            residual_ref[pl.ds(t * nz + z, cf, stride=sites), :] = rest[t + 1, z + 1]
+            residual_ref[pl.ds(t * nz + z, cf, stride=sites), :] = r5[t + 2, z + 2]
     arrive(z_copies)
+    z_edges(0, r4, r5)
     for places in (columns[0], columns[-1]):
-        outer_z(last, places[0][1])
         for t, z in places:
-            residual_ref[pl.ds(t * nz + z, cf, stride=sites), :] = rest[t + 1, z + 1]
+            residual_ref[pl.ds(t * nz + z, cf, stride=sites), :] = r5[t + 2, z + 2]
     for copy in pending:
         copy.wait_send()
 
@@ -420,18 +397,13 @@
             in_specs=[hbm] * len(operands),
             out_specs=(vmem, vmem),
             scratch_shapes=[pltpu.VMEM(operand.shape, operand.dtype) for operand in operands] + [
-                pltpu.VMEM((5, nt + 4, nz + 4, cf, plane), F32),
+                pltpu.VMEM((7, nt + 4, nz + 4, cf, plane), F32),
                 pltpu.VMEM((1 + SWEEPS, nt + 4, nz + 4, cplane, cc), F32),
-                pltpu.VMEM((nt, nz, cf, plane), F32),
-                pltpu.VMEM((nt + 2, nz + 2, cf, plane), F32),
                 pltpu.VMEM((nt + 2, nz + 2, 8, plane), F32),
                 pltpu.VMEM((crows, cc), F32),
-                pltpu.VMEM((2 * cf, 5 * cf), BF16),
-                pltpu.VMEM((2 * cf, 4 * cf), BF16),
-                pltpu.VMEM((2 * cf, 2 * cf), BF16),
-                pltpu.VMEM((2 * cf, 2 * cf), BF16),
-                pltpu.VMEM((2 * cf, cf), BF16),
-                pltpu.VMEM((2 * cf, cf), BF16),
+                pltpu.VMEM((2, 2 * cf, 9 * cf), BF16),
+                pltpu.VMEM((2, 2 * cf, 8 * cf), BF16),
+                pltpu.VMEM((2, 4, 2 * cf, cf), BF16),
                 pltpu.VMEM((2 * cf, cf), BF16),
                 pltpu.VMEM((2 * plane, 4 * plane), BF16),
                 pltpu.VMEM((2 * crows, sites * plane), BF16),

time: 77.4 us -> 75.2 us (0.972)
  Pallas kernels: 73.6 us -> 71.4 us
    pallas_call x1, Pallas kernels: 73.6 us -> 71.4 us  [shards(): pl.pallas_call(functools.partial(kernel, sizes), out_shape=(out, out), in...]
where the time goes in v2:
time: 75.2 us; the launch traced here: 75.1 us
  Pallas kernels  71.4 us (95%)
  local copies, waits for them, and re-layouts  3.02 us (4%)
    pallas_call x1, Pallas kernels, shards(): pl.pallas_call(functools.partial(kernel, sizes), out_shape=(out, out), in...  71.4 us
    unnamed x4, local copies, waits for them, and re-layouts  3.02 us

profile of v2, /device:TPU:0, one launch (start us, length us, event | category | flops | bytes accessed | tf_op | source)
XLA Modules:
  0.0 75.1 jit_solution(489982936447933965)
XLA Ops:
  0.6 71.4 %shard_map.122 = (f32[1536,128]{1,0:T(8,128)}, f32[1536,128]{1,0:T(8,128)}) custom-call(f32[1536,128]{1,0:T(8,128)} %bitcast.6, f32[128,128]{1,0:T(8,128)} %bitcast.9, f32[9,96,96]{2,1,0:T(8,128)} %blocks_hbm.1, f32[96,96]{1,0:T(8,128)} %smoother_hbm.1, s32[4,128]{1,0:T(4,128)} %next_hbm.1, s32[1,128]{1,0:T(1,128)} %bitcast.11, f32[96,128]{1,0:T(8,128)} %restrict_hbm.1, ...), custom_call_target="tpu_custom_call" | custom-call | tf_op jit(solution)/shard_map/pallas_call | solution.py:394
  72.0 0.0 copy-start
  72.0 2.1 %copy.15 = f32[1,96,4,4,128]{4,3,2,1,0:T(4,128)} copy(f32[1,96,4,4,128]{4,3,2,1,0:T(4,128)} %bitcast.8) | data formatting | bytes 1572864
  74.2 0.0 copy-done
  74.2 0.9 %copy.16 = f32[1,96,4,4,128]{4,3,2,1,0:T(4,128)} copy(f32[1,96,4,4,128]{4,3,2,1,0:T(4,128)S(1)} %bitcast.7) | data formatting | bytes 1572864
Async XLA Ops:
  72.0 2.1 %copy-start = (f32[1536,128]{1,0:T(8,128)S(1)}, f32[1536,128]{1,0:T(8,128)}, u32[]{:S(2)}) copy-start(f32[1536,128]{1,0:T(8,128)} %get-tuple-element.5) | copy-start | bytes 2359300

commit v3 on v2

--- a/solution.py
+++ b/solution.py
@@ -99,14 +99,16 @@
         pending.append(copy)
         return copy
 
+    def send_low(buffer, number, pad, width=1):
+        inner, low, above = pl.ds(pad, nt), pl.ds(pad, width), pl.ds(pad + nz, width)
+        return [send(number, 0, buffer.at[inner, low], buffer.at[inner, above], z_before)]
+
+    def send_high(buffer, number, pad, width=1):
+        inner, high, below = pl.ds(pad, nt), pl.ds(pad + nz - width, width), pl.ds(pad - width, width)
+        return [send(number, 1, buffer.at[inner, high], buffer.at[inner, below], z_after)]
+
     def send_z(buffer, number, pad, width=1):
-        inner = pl.ds(pad, nt)
-        low, high = pl.ds(pad, width), pl.ds(pad + nz - width, width)
-        above, below = pl.ds(pad + nz, width), pl.ds(pad - width, width)
-        return [
-            send(number, 0, buffer.at[inner, low], buffer.at[inner, above], z_before),
-            send(number, 1, buffer.at[inner, high], buffer.at[inner, below], z_after),
-        ]
+        return send_low(buffer, number, pad, width) + send_high(buffer, number, pad, width)
 
     def send_t(buffer, number, pad, width=1):
         inner = pl.ds(pad, nz)
@@ -195,8 +197,10 @@
     for z in edges_first:
         for t in range(nt):
             r0[t + 2, z + 2] = rhs_ref[pl.ds(t * nz + z, cf, stride=sites), :]
+        if z == 0:
+            z_copies = send_low(r0, 0, 2)
         if z == nz - 1:
-            z_copies = send_z(r0, 0, 2)
+            z_copies += send_high(r0, 0, 2)
     t_copies = send_t(r0, 0, 2)
 
     for name in ("smoother", "weights", "blocks", "next"):
@@ -204,7 +208,6 @@
     for t in range(nt):
         for z in range(nz):
             weights[t + 1, z + 1] = weight_ref[pl.ds(t * nz + z, 8, stride=sites), :]
-    weight_copies = send_z(weights, 4, 1) + send_t(weights, 4, 1)
     smooth_pair[...] = stacked(smoother_ref[...], 0)
     blocks = [blocks_ref[k] for k in range(9)]
     smoothed = lax.dot_general(
@@ -259,8 +262,10 @@
     arrive(t_copies)
     t_edges(0, r0, r1)
     arrive(z_copies)
-    z_edges(0, r0, r1)
-    z_copies = send_z(r1, 1, 2)
+    edge(0, r0, r1, 4, columns[0])
+    z_copies = send_low(r1, 1, 2)
+    edge(0, r0, r1, 3, columns[-1])
+    z_copies += send_high(r1, 1, 2)
     t_copies = send_t(r1, 1, 2)
     local_terms(0, r1, r1, r2)
     arrive(t_copies)
@@ -268,7 +273,24 @@
     arrive(z_copies)
     z_edges(0, r1, r2)
 
-    rest_copies = send_z(r2, 2, 2) + send_t(r2, 2, 2)
+    pieces = 1 + SWEEPS
+
+    def send_piece(piece):
+        number = 6 + SWEEPS + piece
+        copies = []
+        for count, build in ((nt, lambda part: (
+            (0, (part, 2), (part, 2 + nz), z_before), (1, (part, 1 + nz), (part, 1), z_after),
+        )), (nz, lambda part: (
+            (2, (2, part), (2 + nt, part), t_before), (3, (1 + nt, part), (1, part), t_after),
+        ))):
+            begin, end = count * piece // pieces, count * (piece + 1) // pieces
+            if begin < end:
+                for index, source, target, device in build(pl.ds(2 + begin, end - begin)):
+                    copies.append(send(number, index, r2.at[source], r2.at[target], device))
+        return copies
+
+    rest_copies = send_piece(0)
+    weight_copies = send_z(weights, 4, 1) + send_t(weights, 4, 1)
 
     line = lax.broadcasted_iota(jnp.int32, (2 * cplane, plane), 0)
     gather = jnp.where(line == aggregate_ref[...], 1.0, 0.0).astype(BF16)
@@ -295,6 +317,7 @@
         buffer = values.at[sweep]
         put(buffer, current)
         copies = send_z(buffer, 5 + sweep, 2) + send_t(buffer, 5 + sweep, 2)
+        rest_copies += send_piece(1 + sweep)
         moved = dot(coarse_shuffle[...], stacked(current, 0))
         terms = [current] + [moved[k * crows:(k + 1) * crows] for k in range(4)]
         rest_coarse = coarse_rhs[...] - right_product(
@@ -341,8 +364,10 @@
 
     for z in edges_first:
         all_terms(0, r3, r3, r4, columns[z])
+        if z == 0:
+            z_copies = send_low(r4, 3, 2)
         if z == nz - 1:
-            z_copies = send_z(r4, 3, 2)
+            z_copies += send_high(r4, 3, 2)
     t_copies = send_t(r4, 3, 2)
     local_terms(0, r4, r4, r5)
     for places in rows:
@@ -414,8 +439,8 @@
                 pltpu.VMEM((cc, 2 * cc), BF16),
                 pltpu.VMEM((4 * crows, 2 * crows), BF16),
                 pltpu.SemaphoreType.DMA((len(operands),)),
-                pltpu.SemaphoreType.DMA((6 + SWEEPS, 8)),
-                pltpu.SemaphoreType.DMA((6 + SWEEPS, 8)),
+                pltpu.SemaphoreType.DMA((7 + 2 * SWEEPS, 8)),
+                pltpu.SemaphoreType.DMA((7 + 2 * SWEEPS, 8)),
             ],
             compiler_params=pltpu.CompilerParams(
                 collective_id=0, has_side_effects=True, vmem_limit_bytes=63 * 1024 * 1024

time: 75.2 us -> 69 us (0.918); the launches traced: 75.1 us -> 68 us
  Pallas kernels: 71.4 us -> 64.3 us
    pallas_call x1, Pallas kernels: 71.4 us -> 64.3 us  [shards(): pl.pallas_call(functools.partial(kernel, sizes), out_shape=(out, out), in...]
where the time goes in v3:
time: 69 us; the launch traced here: 68 us
  Pallas kernels  64.3 us (93%)
  local copies, waits for them, and re-layouts  3.02 us (4%)
    pallas_call x1, Pallas kernels, shards(): pl.pallas_call(functools.partial(kernel, sizes), out_shape=(out, out), in...  64.3 us
    unnamed x4, local copies, waits for them, and re-layouts  3.02 us

profile of v3, /device:TPU:0, one launch (start us, length us, event | category | flops | bytes accessed | tf_op | source)
XLA Modules:
  0.0 68.0 jit_solution(7329830865128186147)
XLA Ops:
  0.6 64.3 %shard_map.122 = (f32[1536,128]{1,0:T(8,128)}, f32[1536,128]{1,0:T(8,128)}) custom-call(f32[1536,128]{1,0:T(8,128)} %bitcast.6, f32[128,128]{1,0:T(8,128)} %bitcast.9, f32[9,96,96]{2,1,0:T(8,128)} %blocks_hbm.1, f32[96,96]{1,0:T(8,128)} %smoother_hbm.1, s32[4,128]{1,0:T(4,128)} %next_hbm.1, s32[1,128]{1,0:T(1,128)} %bitcast.11, f32[96,128]{1,0:T(8,128)} %restrict_hbm.1, ...), custom_call_target="tpu_custom_call" | custom-call | tf_op jit(solution)/shard_map/pallas_call | solution.py:419
  65.0 0.0 copy-start
  65.0 2.1 %copy.15 = f32[1,96,4,4,128]{4,3,2,1,0:T(4,128)} copy(f32[1,96,4,4,128]{4,3,2,1,0:T(4,128)} %bitcast.8) | data formatting | bytes 1572864
  67.1 0.0 copy-done
  67.1 0.9 %copy.16 = f32[1,96,4,4,128]{4,3,2,1,0:T(4,128)} copy(f32[1,96,4,4,128]{4,3,2,1,0:T(4,128)S(1)} %bitcast.7) | data formatting | bytes 1572864
Async XLA Ops:
  65.0 2.1 %copy-start = (f32[1536,128]{1,0:T(8,128)S(1)}, f32[1536,128]{1,0:T(8,128)}, u32[]{:S(2)}) copy-start(f32[1536,128]{1,0:T(8,128)} %get-tuple-element.5) | copy-start | bytes 2359300

commit v4 on v3

--- a/solution.py
+++ b/solution.py
@@ -267,6 +267,7 @@
     edge(0, r0, r1, 3, columns[-1])
     z_copies += send_high(r1, 1, 2)
     t_copies = send_t(r1, 1, 2)
+    weight_copies = send_z(weights, 4, 1) + send_t(weights, 4, 1)
     local_terms(0, r1, r1, r2)
     arrive(t_copies)
     t_edges(0, r1, r2)
@@ -290,7 +291,6 @@
         return copies
 
     rest_copies = send_piece(0)
-    weight_copies = send_z(weights, 4, 1) + send_t(weights, 4, 1)
 
     line = lax.broadcasted_iota(jnp.int32, (2 * cplane, plane), 0)
     gather = jnp.where(line == aggregate_ref[...], 1.0, 0.0).astype(BF16)

time: 69 us -> 69.1 us (level); the launches traced: 68 us -> 68.9 us
  Pallas kernels: 64.3 us -> 65.3 us
    pallas_call x1, Pallas kernels: 64.3 us -> 65.3 us  [shards(): pl.pallas_call(functools.partial(kernel, sizes), out_shape=(out, out), in...]
where the time goes in v4:
time: 69.1 us; the launch traced here: 68.9 us
  Pallas kernels  65.3 us (95%)
  local copies, waits for them, and re-layouts  3.02 us (4%)
    pallas_call x1, Pallas kernels, shards(): pl.pallas_call(functools.partial(kernel, sizes), out_shape=(out, out), in...  65.3 us
    unnamed x4, local copies, waits for them, and re-layouts  3.02 us

profile of v4, /device:TPU:0, one launch (start us, length us, event | category | flops | bytes accessed | tf_op | source)
XLA Modules:
  0.0 68.9 jit_solution(14387936591493840719)
XLA Ops:
  0.6 65.3 %shard_map.122 = (f32[1536,128]{1,0:T(8,128)}, f32[1536,128]{1,0:T(8,128)}) custom-call(f32[1536,128]{1,0:T(8,128)} %bitcast.6, f32[128,128]{1,0:T(8,128)} %bitcast.9, f32[9,96,96]{2,1,0:T(8,128)} %blocks_hbm.1, f32[96,96]{1,0:T(8,128)} %smoother_hbm.1, s32[4,128]{1,0:T(4,128)} %next_hbm.1, s32[1,128]{1,0:T(1,128)} %bitcast.11, f32[96,128]{1,0:T(8,128)} %restrict_hbm.1, ...), custom_call_target="tpu_custom_call" | custom-call | tf_op jit(solution)/shard_map/pallas_call | solution.py:419
  65.9 0.0 copy-start
  65.9 2.1 %copy.15 = f32[1,96,4,4,128]{4,3,2,1,0:T(4,128)} copy(f32[1,96,4,4,128]{4,3,2,1,0:T(4,128)} %bitcast.8) | data formatting | bytes 1572864
  68.0 0.0 copy-done
  68.0 0.9 %copy.16 = f32[1,96,4,4,128]{4,3,2,1,0:T(4,128)} copy(f32[1,96,4,4,128]{4,3,2,1,0:T(4,128)S(1)} %bitcast.7) | data formatting | bytes 1572864
Async XLA Ops:
  65.9 2.1 %copy-start = (f32[1536,128]{1,0:T(8,128)S(1)}, f32[1536,128]{1,0:T(8,128)}, u32[]{:S(2)}) copy-start(f32[1536,128]{1,0:T(8,128)} %get-tuple-element.5) | copy-start | bytes 2359300
